TPU v7x, 32 devices: a whole 2x2x4 slice. The times are simulated.
32 devices in a mesh: seq: 8 (over y, x, core), chan: 4 (over z).
Axes of the slice: x: 2, y: 2, z: 4, core: 2. Of those that a mesh axis runs over, the one named last changes fastest.
Arguments:
- query_rows: bfloat16 [1024, 8192], P('seq', 'chan'), may hold values from -6 to 6
- key_rows: bfloat16 [1024, 8192], P('seq', 'chan'), may hold values from -6 to 6
- value_rows: bfloat16 [1024, 8192], P('seq', 'chan'), may hold values from -6 to 6
- grad_rows: bfloat16 [1024, 8192], P('seq', 'chan'), may hold values from -21 to 21
- filters: bfloat16 [512, 128], P('chan'), may hold values from -0.5 to 0.5
- span_order: int32 [16], replicated, may hold values from 0 to 15, as said below
Outputs:
- gated_out: bfloat16 [1024, 8192], P('seq', 'chan')
- grad_query: bfloat16 [1024, 8192], P('seq', 'chan')
- grad_key: bfloat16 [1024, 8192], P('seq', 'chan')
- grad_value: bfloat16 [1024, 8192], P('seq', 'chan')
- filter_grad: float32 [512, 128], P('chan')
Inputs may be any that keep to these rules, and one draw needn't show every extreme that they name: span_order names every span once. Slot s lies on seq index s // 2, and span c is owned by seq index c // 2. Seq index i holds a span p below 8 in slot 2 * i and span 16 - 1 - p in slot 2 * i + 1; which p each index holds is drawn. No seq index holds two spans of one owner.
All inputs are finite; a program needn't handle non-finite values.
Results may differ from a plain program's by a relative error of at most 0.0085.
Values may be sent and summed in bfloat16 or wider, within the bound.
A program may use at most 128 MiB of HBM per device.

v0:
```python
import math

import jax
import jax.numpy as jnp
import numpy as np
from jax import lax
from jax.sharding import PartitionSpec as P

CPD = 2
MOST = 1


def from_behind(array, axis, by):
    size = lax.axis_size(axis)
    pairs = [(i, i + by) for i in range(size) if 0 <= i + by < size]
    return lax.ppermute(array, axis, pairs)


def band_tables(filters):
    taps = filters.shape[1]
    offsets = (np.arange(taps)[:, None] - np.arange(taps)[None, :]) % taps
    below = np.arange(taps)[:, None] >= np.arange(taps)[None, :]
    lookup = filters[:, offsets]
    zeroed = jnp.zeros_like(lookup)
    return (jnp.where(below, lookup, zeroed), jnp.where(below, zeroed, lookup))


def times_rounded(left, right):
    return (left.astype(jnp.float32) * right.astype(jnp.float32)).astype(jnp.bfloat16)


def route_plan(span_order, device, per_device, devices, capacity):
    owner_grid = (span_order // per_device).reshape(devices, per_device)
    position = jnp.arange(per_device, dtype=jnp.int32)
    earlier = (owner_grid[:, :, None] == owner_grid[:, None, :]) & (
        position[None, None, :] < position[None, :, None]
    )
    ranks = jnp.sum(earlier.astype(jnp.int32), axis=2)
    send_key = owner_grid * capacity + ranks
    arrive_key = (jnp.arange(devices, dtype=jnp.int32)[:, None] * capacity + ranks).reshape(-1)
    my_keys = lax.dynamic_index_in_dim(send_key, device, 0, keepdims=False)
    buffer_slots = jnp.arange(devices * capacity, dtype=jnp.int32)
    hits = my_keys[None, :] == buffer_slots[:, None]
    fill_slot = jnp.sum(jnp.where(hits, position[None, :], 0), axis=1)
    fill_valid = jnp.any(hits, axis=1)
    wanted = device * per_device + position
    owned = span_order[None, :] == wanted[:, None]
    take_slot = jnp.sum(jnp.where(owned, arrive_key[None, :], 0), axis=1)
    back_hits = take_slot[None, :] == buffer_slots[:, None]
    back_slot = jnp.sum(jnp.where(back_hits, position[None, :], 0), axis=1)
    back_valid = jnp.any(back_hits, axis=1)
    return (fill_slot, fill_valid, take_slot, back_slot, back_valid, my_keys)


def pack_rows(block, slot_index, valid, per_device):
    channels = block.shape[1]
    pieces = block.reshape(per_device, -1, channels)
    picked = jnp.take(pieces, slot_index, axis=0)
    picked = jnp.where(valid[:, None, None], picked, jnp.zeros_like(picked))
    return picked.reshape(-1, channels)


def unpack_rows(received, slot_index, count):
    channels = received.shape[1]
    pieces = received.reshape(count, -1, channels)
    return jnp.take(pieces, slot_index, axis=0).reshape(-1, channels)


def forward_conv(source, tail_rows, main_band, wrap_band, group_size):
    taps = main_band.shape[1]
    row_count, channels = source.shape
    extended = jnp.concatenate([jnp.zeros((1, channels), source.dtype), tail_rows, source], axis=0)
    tile_grid = extended.reshape(row_count // taps + 1, taps, channels // group_size, group_size)
    result = jnp.einsum(
        "gab,tbgc->tagc", main_band, tile_grid[1:], preferred_element_type=jnp.float32
    )
    result = result + jnp.einsum(
        "gab,tbgc->tagc", wrap_band, tile_grid[:-1], preferred_element_type=jnp.float32
    )
    return (result.reshape(row_count, channels), tile_grid)


def backward_conv(source, head_rows, main_band, wrap_band, group_size):
    taps = main_band.shape[1]
    row_count, channels = source.shape
    extended = jnp.concatenate([source, head_rows, jnp.zeros((1, channels), source.dtype)], axis=0)
    tile_grid = extended.reshape(row_count // taps + 1, taps, channels // group_size, group_size)
    result = jnp.einsum(
        "gba,tbgc->tagc", main_band, tile_grid[:-1], preferred_element_type=jnp.float32
    )
    result = result + jnp.einsum(
        "gba,tbgc->tagc", wrap_band, tile_grid[1:], preferred_element_type=jnp.float32
    )
    return result.reshape(row_count, channels)


def filter_terms(gated_grad, z_grid, group_size):
    taps = z_grid.shape[1]
    tile_count = z_grid.shape[0] - 1
    grad_tiles = gated_grad.reshape(tile_count, taps, -1, group_size)
    windows = jnp.concatenate([z_grid[:-1], z_grid[1:]], axis=1)
    products = jnp.einsum("tagc,tbgc->gab", grad_tiles, windows, preferred_element_type=jnp.float32)
    groups = products.shape[0]
    flattened = products.reshape(groups, 2 * taps * taps)
    padded = jnp.concatenate([flattened, jnp.zeros((groups, taps), jnp.float32)], axis=1)
    padded = padded.reshape(groups, taps, 2 * taps + 1)
    diagonals = jnp.sum(padded[:, :, 1 : taps + 1], axis=1)
    return diagonals[:, ::-1]


def shards(query_rows, key_rows, value_rows, grad_rows, filters, span_order):
    device = lax.axis_index("seq")
    devices = lax.axis_size("seq")
    row_count = query_rows.shape[0]
    taps = filters.shape[1]
    group_size = query_rows.shape[1] // filters.shape[0]
    capacity = MOST
    per_device = CPD
    slot_total = devices * capacity
    fill_slot, fill_valid, take_slot, back_slot, back_valid, my_keys = route_plan(
        span_order, device, per_device, devices, capacity
    )
    main_band, wrap_band = band_tables(filters)
    moved = (
        lax.all_to_all(
            pack_rows(query_rows, fill_slot, fill_valid, per_device),
            "seq",
            split_axis=0,
            concat_axis=0,
            tiled=True,
        ),
        lax.all_to_all(
            pack_rows(key_rows, fill_slot, fill_valid, per_device),
            "seq",
            split_axis=0,
            concat_axis=0,
            tiled=True,
        ),
        lax.all_to_all(
            pack_rows(value_rows, fill_slot, fill_valid, per_device),
            "seq",
            split_axis=0,
            concat_axis=0,
            tiled=True,
        ),
        lax.all_to_all(
            pack_rows(grad_rows, fill_slot, fill_valid, per_device),
            "seq",
            split_axis=0,
            concat_axis=0,
            tiled=True,
        ),
    )
    owner_query = unpack_rows(moved[0], take_slot, slot_total)
    owner_key = unpack_rows(moved[1], take_slot, slot_total)
    owner_value = unpack_rows(moved[2], take_slot, slot_total)
    owner_grad = unpack_rows(moved[3], take_slot, slot_total)
    mixed_kv = times_rounded(owner_key, owner_value)
    gated_grad = times_rounded(owner_grad, owner_query)
    tail_rows = from_behind(mixed_kv[row_count - taps + 1 :], "seq", 1)
    head_rows = from_behind(gated_grad[: taps - 1], "seq", -1)
    conv, z_grid = forward_conv(mixed_kv, tail_rows, main_band, wrap_band, group_size)
    convolved = conv.astype(jnp.bfloat16)
    dmixed = backward_conv(gated_grad, head_rows, main_band, wrap_band, group_size).astype(
        jnp.bfloat16
    )
    partial_grad = filter_terms(gated_grad, z_grid, group_size)
    total_grad = lax.psum(partial_grad, "seq")
    squares = lax.psum(jnp.sum(total_grad * total_grad), "chan")
    limit = math.sqrt(filters.shape[0] * lax.axis_size("chan") * taps)
    factor = jnp.minimum(1.0, limit * lax.rsqrt(squares + 1e-06))
    filter_grad = factor * total_grad
    returned = (
        lax.all_to_all(
            pack_rows(times_rounded(owner_query, convolved), back_slot, back_valid, per_device),
            "seq",
            split_axis=0,
            concat_axis=0,
            tiled=True,
        ),
        lax.all_to_all(
            pack_rows(times_rounded(owner_grad, convolved), back_slot, back_valid, per_device),
            "seq",
            split_axis=0,
            concat_axis=0,
            tiled=True,
        ),
        lax.all_to_all(
            pack_rows(times_rounded(dmixed, owner_value), back_slot, back_valid, per_device),
            "seq",
            split_axis=0,
            concat_axis=0,
            tiled=True,
        ),
        lax.all_to_all(
            pack_rows(times_rounded(dmixed, owner_key), back_slot, back_valid, per_device),
            "seq",
            split_axis=0,
            concat_axis=0,
            tiled=True,
        ),
    )
    gated_out = unpack_rows(returned[0], my_keys, slot_total)
    grad_query = unpack_rows(returned[1], my_keys, slot_total)
    grad_key = unpack_rows(returned[2], my_keys, slot_total)
    grad_value = unpack_rows(returned[3], my_keys, slot_total)
    return (gated_out, grad_query, grad_key, grad_value, filter_grad)


def solution(mesh):
    return jax.shard_map(
        shards,
        mesh=mesh,
        in_specs=(
            P("seq", "chan"),
            P("seq", "chan"),
            P("seq", "chan"),
            P("seq", "chan"),
            P("chan", None),
            P(),
        ),
        out_specs=(
            P("seq", "chan"),
            P("seq", "chan"),
            P("seq", "chan"),
            P("seq", "chan"),
            P("chan", None),
        ),
        check_vma=False,
    )
```

profile of v0, /device:TPU:0, one launch (start us, length us, event | category | flops | bytes accessed | tf_op | source)
XLA Modules:
  0.0 483.1 jit_solution(11729067336899197623)
XLA Ops:
  15.7 4.7 select_select_fusion.3
  20.4 31.6 %all_to_all.48 = bf16[8,64,2048]{2,1,0:T(8,128)(2,1)S(1)} all-to-all(bf16[8,64,2048]{2,1,0:T(8,128)(2,1)S(1)} %get-tuple-element.31), channel_id=1, replica_groups=mesh['seq'=8,'chan'=4] {'seq'}, dimensions={0} | all-to-all | bytes 4194304 | tf_op jit(solution)/shard_map/all_to_all | solution.py:146
  51.9 29.8 %all_to_all.49 = bf16[8,64,2048]{2,1,0:T(8,128)(2,1)} all-to-all(bf16[8,64,2048]{2,1,0:T(8,128)(2,1)S(1)} %get-tuple-element.32), channel_id=1, replica_groups=mesh['seq'=8,'chan'=4] {'seq'}, dimensions={0} | all-to-all | bytes 4194304 | tf_op jit(solution)/shard_map/all_to_all | solution.py:132
  81.7 4.5 all-to-all-start
  86.5 57.4 %gather_fusion = bf16[16384,128]{1,0:T(8,128)(2,1)} fusion(bf16[128,128]{0,1:T(8,128)(2,1)S(1)} %copy.74, s32[16384]{0:T(1024)S(1)} %broadcast_clamp_fusion), kind=kCustom, calls=%fused_computation.16 | custom fusion | bytes 8454144 | tf_op jit(solution)/shard_map/gather | solution.py:23
  143.9 6.6 %copy.75 = bf16[128,128,128]{1,0,2:T(8,128)(2,1)} copy(bf16[128,128,128]{2,1,0:T(8,128)(2,1)} %bitcast.94) | data formatting | bytes 8388608 | tf_op jit(solution)/shard_map/gather | solution.py:23
  150.5 4.5 all-to-all-start.2
  155.9 2.2 gather_fusion.2
  161.0 3.2 gather_fusion.4
  164.1 17.5 %all-to-all-done.2 = bf16[8,64,2048]{2,1,0:T(8,128)(2,1)} async-done(((bf16[8,64,2048]{2,1,0:T(8,128)(2,1)}), bf16[8,64,2048]{2,1,0:T(8,128)(2,1)}, u32[]{:S(2)}, u32[]{:S(2)}) %all-to-all-start.2) | async-done | bytes 2097184 | tf_op jit(solution)/shard_map/all_to_all | solution.py:139
  181.7 3.0 gather_fusion.6
  184.6 3.4 fusion.4
  189.5 4.4 fusion.39
  193.9 2.5 reshape.258
  208.8 5.5 %fusion.6 = f32[128,16,128]{2,1,0:T(8,128)} fusion(bf16[128,128,16]{0,2,1:T(8,128)(2,1)S(1)} %convert_element_type.154, bf16[128,128,128]{1,0,2:T(8,128)(2,1)} %copy.75, pred[128,128]{1,0:T(8,128)(4,1)S(1)} %bitcast.109), kind=kOutput, calls=%fused_computation.24 | convolution fusion | flops 69206016 | bytes 5783552 | tf_op jit(solution)/shard_map/gab,tbgc->tagc/dot_general | solution.py:74
  215.9 6.0 %fusion.30 = f32[1,128,128,16]{1,3,2,0:T(8,128)} fusion(f32[128,16,128]{2,1,0:T(8,128)} %fusion.6, bf16[128,128,16]{0,2,1:T(8,128)(2,1)S(1)} %bitcast.100, bf16[128,128,128]{1,0,2:T(8,128)(2,1)} %copy.75, pred[128,128]{1,0:T(8,128)(4,1)S(1)} %bitcast.110), kind=kOutput, calls=%fused_computation.52 | convolution fusion | flops 69992448 | bytes 6832128 | tf_op jit(solution)/shard_map/gab,tbgc->tagc/dot_general | solution.py:77
  221.8 3.4 reshape.257
  225.2 4.0 copy.78
  234.8 4.9 %select_select_fusion = (bf16[8,64,2048]{2,1,0:T(8,128)(2,1)S(1)}, bf16[8,64,2048]{2,1,0:T(8,128)(2,1)S(1)}, bf16[8,64,2048]{2,1,0:T(8,128)(2,1)S(1)}, bf16[8,64,2048]{2,1,0:T(8,128)(2,1)}) fusion(bf16[8,64,2048]{2,1,0:T(8,128)(2,1)} %gather_fusion.15, pred[8]{0:T(512)(128)(4,1)S(1)} %compare_and_fusion.1, pred[8]{0:T(512)(128)(4,1)S(1)} %fusion.54, ...), kind=kLoop, calls=%fused_computation.28 | loop fusion | flops 8388608 | bytes 16777232 | tf_op jit(solution)/shard_map/jit(_where)/select_n | solution.py:59
  239.7 29.7 %all_to_all.50 = bf16[8,64,2048]{2,1,0:T(8,128)(2,1)} all-to-all(bf16[8,64,2048]{2,1,0:T(8,128)(2,1)S(1)} %get-tuple-element.27), channel_id=1, replica_groups=mesh['seq'=8,'chan'=4] {'seq'}, dimensions={0} | all-to-all | bytes 4194304 | tf_op jit(solution)/shard_map/all_to_all | solution.py:195
  269.5 29.8 %all_to_all.51 = bf16[8,64,2048]{2,1,0:T(8,128)(2,1)} all-to-all(bf16[8,64,2048]{2,1,0:T(8,128)(2,1)S(1)} %get-tuple-element.28), channel_id=1, replica_groups=mesh['seq'=8,'chan'=4] {'seq'}, dimensions={0} | all-to-all | bytes 4194304 | tf_op jit(solution)/shard_map/all_to_all | solution.py:181
  299.2 29.7 %all_to_all.52 = bf16[8,64,2048]{2,1,0:T(8,128)(2,1)} all-to-all(bf16[8,64,2048]{2,1,0:T(8,128)(2,1)S(1)} %get-tuple-element.29), channel_id=1, replica_groups=mesh['seq'=8,'chan'=4] {'seq'}, dimensions={0} | all-to-all | bytes 4194304 | tf_op jit(solution)/shard_map/all_to_all | solution.py:188
  329.0 4.5 all-to-all-start.3
  334.0 8.1 %fusion.48 = f32[128,128,256]{2,1,0:T(8,128)} fusion(bf16[128,128,16]{0,2,1:T(8,128)(2,1)S(1)} %copy-done.8, bf16[1,128,128,16]{1,3,2,0:T(8,128)(2,1)S(1)} %convert_element_type.174, bf16[1,128,128,16]{1,3,2,0:T(8,128)(2,1)S(1)} %bitcast.101), kind=kOutput, calls=%fused_computation.63 | convolution fusion | flops 136314880 | bytes 18350080 | tf_op jit(solution)/shard_map/tagc,tbgc->gab/dot_general | solution.py:102
  342.1 17.8 %copy.88 = f32[128,128,256]{0,2,1:T(8,128)} copy(f32[128,128,256]{2,1,0:T(8,128)} %fusion.48) | data formatting | bytes 33554432 | tf_op jit(solution)/shard_map/reshape | solution.py:104
  359.9 13.3 %concatenate.17 = f32[128,32896]{0,1:T(8,128)} pad(f32[128,32768]{0,1:T(8,128)} %bitcast.93, f32[]{:T(128)} %constant.66.clone.1), padding=0_0x0_128 | pad | bytes 33619972 | tf_op jit(solution)/shard_map/concatenate | solution.py:105
  373.2 17.5 %reshape.256 = f32[128,128,257]{0,2,1:T(8,128)} reshape(f32[128,32896]{0,1:T(8,128)} %concatenate.17) | data formatting | bytes 33685504 | tf_op jit(solution)/shard_map/reshape | solution.py:106
  390.7 4.4 slice_reduce_fusion
  395.8 54.2 %all-reduce.5.cloned.1.call-done = f32[128,128]{0,1:T(8,128)} async-done(((f32[128,128]{0,1:T(8,128)}), f32[128,128]{0,1:T(8,128)}) %all-reduce.5.cloned.1.call-update) | async-done | bytes 65552 | tf_op jit(solution)/shard_map/psum | solution.py:168
  451.5 12.3 %psum.15 = f32[]{:T(128)} all-reduce(f32[]{:T(128)} %multiply_reduce_fusion), channel_id=1, replica_groups=mesh['seq'=8,'chan'=4] {'chan'}, use_global_device_ids=true, to_apply=%region_9.12 | all-reduce | flops 1 | bytes 8 | tf_op jit(solution)/shard_map/psum | solution.py:169
  468.2 2.2 gather_fusion.12
  472.6 2.2 gather_fusion.8
  (97 shorter events, 43.5 us)
Async XLA Ops:
  7.2 1.4 copy-start
  8.6 1.0 copy-start.2
  9.6 2.0 copy-start.3
  11.7 2.0 copy-start.4
  81.7 4.7 copy-start.12
  81.7 4.8 copy-start.11
  81.7 68.8 %all-to-all-start = ((bf16[8,64,2048]{2,1,0:T(8,128)(2,1)}), bf16[8,64,2048]{2,1,0:T(8,128)(2,1)}, u32[]{:S(2)}, u32[]{:S(2)}) async-start(bf16[8,64,2048]{2,1,0:T(8,128)(2,1)} %get-tuple-element.34), calls=%async_computation | async-start | bytes 4194304 | tf_op jit(solution)/shard_map/all_to_all | solution.py:125
  150.5 4.5 copy-start.13
  150.5 31.1 %all-to-all-start.2 = ((bf16[8,64,2048]{2,1,0:T(8,128)(2,1)}), bf16[8,64,2048]{2,1,0:T(8,128)(2,1)}, u32[]{:S(2)}, u32[]{:S(2)}) async-start(bf16[8,64,2048]{2,1,0:T(8,128)(2,1)} %get-tuple-element.33), calls=%async_computation.2 | async-start | bytes 4194304 | tf_op jit(solution)/shard_map/all_to_all | solution.py:139
  158.1 2.9 copy-start.5
  158.4 29.6 %collective-permute-start.1 = (bf16[127,2048]{1,0:T(8,128)(2,1)S(1)}, bf16[127,2048]{1,0:T(8,128)(2,1)}, u32[]{:S(2)}, u32[]{:S(2)}) collective-permute-start(bf16[127,2048]{1,0:T(8,128)(2,1)S(1)} %bitcast.99), channel_id=1, source_target_pairs={{4,0},{8,4},{12,8},{16,12},{20,16},{24,20},{28,24},{5,1},{9,5},{13... | collective-permute-start | bytes 1560584 | tf_op jit(solution)/shard_map/ppermute | solution.py:16
  160.5 24.2 %copy-start.14 = (pred[128,128]{1,0:T(32,128)(4,1)S(1)}, pred[128,128]{1,0:T(32,128)(4,1)}, u32[]{:S(2)}) copy-start(pred[128,128]{1,0:T(32,128)(4,1)} %constant.72.clone) | copy-start | bytes 49156
  161.0 27.0 %copy-start.7 = (bf16[128,128,16]{0,2,1:T(8,128)(2,1)}, bf16[128,128,16]{0,2,1:T(8,128)(2,1)S(1)}, u32[]{:S(2)}) copy-start(bf16[128,128,16]{0,2,1:T(8,128)(2,1)S(1)} %convert_element_type.165) | copy-start | bytes 1572868
  201.4 12.9 %collective-permute-start = (bf16[127,2048]{1,0:T(8,128)(2,1)}, bf16[127,2048]{1,0:T(8,128)(2,1)}, u32[]{:S(2)}, u32[]{:S(2)}) collective-permute-start(bf16[127,2048]{1,0:T(8,128)(2,1)} %slice.61), channel_id=1, source_target_pairs={{0,4},{4,8},{8,12},{12,16},{16,20},{20,24},{24,28},{1,5},{5,9},{9,... | collective-permute-start | bytes 1560584 | tf_op jit(solution)/shard_map/ppermute | solution.py:16
  215.8 6.0 %copy-start.9 = (bf16[128,2048]{0,1:T(8,128)(2,1)}, bf16[128,2048]{0,1:T(8,128)(2,1)S(1)}, u32[]{:S(2)}) copy-start(bf16[128,2048]{0,1:T(8,128)(2,1)S(1)} %concatenate.14.clone) | copy-start | bytes 1572868
  225.2 4.0 copy-start.6
  329.0 5.0 %copy-start.8 = (bf16[128,128,16]{0,2,1:T(8,128)(2,1)S(1)}, bf16[128,128,16]{0,2,1:T(8,128)(2,1)}, u32[]{:S(2)}) copy-start(bf16[128,128,16]{0,2,1:T(8,128)(2,1)} %copy-done.7) | copy-start | bytes 1572868
  329.0 5.0 %copy-start.10 = (bf16[128,2048]{0,1:T(8,128)(2,1)S(1)}, bf16[128,2048]{0,1:T(8,128)(2,1)}, u32[]{:S(2)}) copy-start(bf16[128,2048]{0,1:T(8,128)(2,1)} %copy-done.9) | copy-start | bytes 1572868
  329.0 143.6 %all-to-all-start.3 = ((bf16[8,64,2048]{2,1,0:T(8,128)(2,1)}), bf16[8,64,2048]{2,1,0:T(8,128)(2,1)}, u32[]{:S(2)}, u32[]{:S(2)}) async-start(bf16[8,64,2048]{2,1,0:T(8,128)(2,1)} %get-tuple-element.30), calls=%async_computation.3 | async-start | bytes 4194304 | tf_op jit(solution)/shard_map/all_to_all | solution.py:174
  333.4 116.6 %all-reduce.5.cloned.1.call-start = ((), (), s32[]{:S(2)}) async-start(), calls=%async_computation.8 | async-start | bytes 131072 | tf_op jit(solution)/shard_map/psum | solution.py:168
  472.6 3.7 copy-start.1
Sparse Core Ops, SparseCore 0:
  395.9 54.0 all-reduce.4
where the time goes:
time: 485 us; the launch traced here: 483 us
  local copies, waits for them, and re-layouts  166 us (34%)
  blocking collectives  163 us (34%)
  waiting for transfers between devices  71.7 us (15%)
  matrix products  27.3 us (6%)
  other arithmetic  23 us (5%)
  starting transfers between devices  16.8 us (3%)
  between operations  15.1 us (3%)
    gather x2, local copies, waits for them, and re-layouts, band_tables(): lookup = filters[:, offsets]  64 us
    psum x1, waiting for transfers between devices, shards(): total_grad = lax.psum(partial_grad, 'seq')  54.2 us
    all_to_all x1, blocking collectives, shards(): lax.all_to_all(pack_rows(grad_rows, fill_slot, fill_valid, per_device), '...  31.6 us
    all_to_all x1, blocking collectives, shards(): lax.all_to_all(pack_rows(key_rows, fill_slot, fill_valid, per_device), 's...  29.8 us
    all_to_all x1, blocking collectives, shards(): lax.all_to_all(pack_rows(times_rounded(owner_grad, convolved), back_slot,...  29.8 us
    all_to_all x1, blocking collectives, shards(): lax.all_to_all(pack_rows(times_rounded(dmixed, owner_key), back_slot, bac...  29.7 us
    all_to_all x1, blocking collectives, shards(): lax.all_to_all(pack_rows(times_rounded(dmixed, owner_value), back_slot, b...  29.7 us
    reshape x1, local copies, waits for them, and re-layouts, filter_terms(): flattened = products.reshape(groups, 2 * taps * taps)  17.8 us
  transfers between devices with their start and end apart: 6, of which 2 were waited for; matrix products, arithmetic and copies ran while one was open for 33% of the time, Pallas kernels for 0%

commit v1 on v0

v1 whole, which is shorter than its diff:
```python
import functools
import math

import jax
import jax.numpy as jnp
from jax import lax
from jax.experimental import pallas as pl
from jax.experimental.pallas import tpu as pltpu
from jax.sharding import PartitionSpec as P

MESH = pl.DeviceIdType.MESH


def flip_bits(me, r, size):
    peer = me
    bit = 1
    while bit < size:
        if r & bit:
            peer = peer + bit - 2 * bit * (lax.div(me, bit) % 2)
        bit *= 2
    return peer


def kernel(
    n, m, taps, group, limit,
    order_ref, slot_ref, base_ref, q_ref, k_ref, v_ref, g_ref,
    go_ref, gq_ref, gk_ref, gv_ref, fg_ref,
    mix_send, gat_send, mix_recv, gat_recv, zseq, gseq, conv, dmix,
    conv_send, dmix_send, conv_ret, dmix_ret, bands, eacc, raws, norms,
    send_sem, recv_sem, norm_send, norm_recv,
):
    me = lax.axis_index("seq")
    line = lax.axis_index("chan")
    spans, span_rows, cw = mix_send.shape
    pd = spans // n
    rows = pd * span_rows
    _, halves, _, lanes = conv.shape
    tokens = spans * span_rows
    tiles = tokens // taps
    window = 2 * taps
    per_half = lanes // group
    groups = halves * per_half
    pair = 2 if lanes == 128 and tiles % 2 == 0 else 1
    steps = tiles // pair
    per_tile = taps // span_rows
    peers = sorted(range(1, n), key=lambda r: (r & 1, -bin(r).count("1")))

    barrier = pltpu.get_barrier_semaphore()
    for r in peers:
        pl.semaphore_signal(
            barrier, inc=1, device_id={"seq": flip_bits(me, r, n)}, device_id_type=MESH
        )
    for r in range(1, m):
        pl.semaphore_signal(
            barrier, inc=1, device_id={"chan": flip_bits(line, r, m)}, device_id_type=MESH
        )

    def exchange(kind, r, source, target):
        return pltpu.make_async_remote_copy(
            src_ref=source,
            dst_ref=target,
            send_sem=send_sem.at[kind, r],
            recv_sem=recv_sem.at[kind, r],
            device_id={"seq": flip_bits(me, r, n)},
            device_id_type=MESH,
        )

    def outward(kind, r, source, target):
        peer = flip_bits(me, r, n)
        return exchange(
            kind, r, source.at[pl.ds(peer * pd, pd)], target.at[pl.ds(me * pd, pd)]
        )

    def to_all(kind, r):
        return exchange(kind, r, raws.at[me], raws.at[me])

    def norm_copy(r):
        return pltpu.make_async_remote_copy(
            src_ref=norms.at[line],
            dst_ref=norms.at[line],
            send_sem=norm_send.at[r],
            recv_sem=norm_recv.at[r],
            device_id={"chan": flip_bits(line, r, m)},
            device_id_type=MESH,
        )

    def blocks(left, right, out):
        for d in range(n):
            cut = slice(d * cw, (d + 1) * cw)
            out[d * pd : (d + 1) * pd] = (left[:, cut] * right[:, cut]).reshape(pd, span_rows, cw)

    blocks(k_ref, v_ref, mix_send)
    pl.semaphore_wait(barrier, n + m - 2)
    for r in peers:
        outward(0, r, mix_send, mix_recv).start()
    blocks(g_ref, q_ref, gat_send)
    for r in peers:
        outward(1, r, gat_send, gat_recv).start()
    mix_recv[pl.ds(me * pd, pd)] = mix_send[pl.ds(me * pd, pd)]
    gat_recv[pl.ds(me * pd, pd)] = gat_send[pl.ds(me * pd, pd)]

    def build_band(i, carry):
        row = base_ref[pl.ds(i, 1), :]
        table = pltpu.roll(
            jnp.broadcast_to(row, (taps, window)), 0, 1, stride=1, stride_axis=0
        )
        bands[i] = table.astype(jnp.bfloat16)
        return carry

    lax.fori_loop(0, 2 * groups, build_band, 0)
    for h in range(halves):
        zseq[h, 0:taps] = jnp.zeros((taps, lanes), jnp.bfloat16)
        gseq[h, tokens : tokens + taps] = jnp.zeros((taps, lanes), jnp.bfloat16)

    column = lax.broadcasted_iota(jnp.int32, (taps, pair * lanes), 1)
    mine = [(column % lanes) // group == i for i in range(per_half)]

    def in_order(source, target, start):
        def step(c, carry):
            block = source[slot_ref[c]]
            at = pl.multiple_of(start + c * span_rows, span_rows)
            for h in range(halves):
                target[h, pl.ds(at, span_rows), :] = block[:, h * lanes : (h + 1) * lanes]
            return carry

        lax.fori_loop(0, spans, step, 0)

    def windows(source, h, u, length):
        parts = [
            source[h, pl.ds(pl.multiple_of((u * pair + p) * taps, taps), length), :]
            for p in range(pair)
        ]
        return parts[0] if pair == 1 else jnp.concatenate(parts, axis=1)

    def convolve(source, first_band, target):
        def step(i, carry):
            h, u = i // steps, i % steps
            weights = windows(source, h, u, window)
            total = jnp.zeros((taps, pair * lanes), jnp.float32)
            for g in range(per_half):
                part = jnp.dot(
                    bands[first_band + h * per_half + g], weights,
                    preferred_element_type=jnp.float32,
                )
                total = jnp.where(mine[g], part, total)
            total = total.astype(jnp.bfloat16)
            for p in range(pair):
                for b in range(per_tile):
                    target[(u * pair + p) * per_tile + b, h] = total[
                        b * span_rows : (b + 1) * span_rows, p * lanes : (p + 1) * lanes
                    ]
            return carry

        lax.fori_loop(0, halves * steps, step, 0)

    def in_slots(source, target):
        def step(s, carry):
            block = source[order_ref[s]]
            for h in range(halves):
                target[s, :, h * lanes : (h + 1) * lanes] = block[h]
            return carry

        lax.fori_loop(0, spans, step, 0)

    def send_back(kind, source, target):
        for r in peers:
            outward(kind, r, source, target).start()
        target[pl.ds(me * pd, pd)] = source[pl.ds(me * pd, pd)]

    for r in peers:
        outward(0, r, mix_send, mix_recv).wait_recv()
    in_order(mix_recv, zseq, taps)
    convolve(zseq, 0, conv)
    in_slots(conv, conv_send)
    send_back(2, conv_send, conv_ret)

    for r in peers:
        outward(1, r, gat_send, gat_recv).wait_recv()
    in_order(gat_recv, gseq, 0)
    convolve(gseq, groups, dmix)
    in_slots(dmix, dmix_send)
    send_back(3, dmix_send, dmix_ret)

    zero = jnp.zeros((taps, pair * lanes), jnp.bfloat16)
    row_at = lax.broadcasted_iota(jnp.int32, (per_half, 8, window), 1)
    for h in range(halves):
        eacc[...] = jnp.zeros_like(eacc)

        def correlate(u, carry):
            parts = [
                zseq[h, pl.ds(pl.multiple_of((u * pair + p + 1) * taps, taps), taps), :]
                for p in range(pair)
            ]
            here = parts[0] if pair == 1 else jnp.concatenate(parts, axis=1)
            ahead = windows(gseq, h, u, window)
            for g in range(per_half):
                eacc[g] += lax.dot_general(
                    jnp.where(mine[g], here, zero), ahead,
                    (((1,), (1,)), ((), ())), preferred_element_type=jnp.float32,
                )
            return carry

        lax.fori_loop(0, steps, correlate, 0)
        half = taps // 2
        left = eacc[...]
        while half >= 8:
            left = left[:, :half] + pltpu.roll(left[:, half:], window - half, 2)
            half //= 2
        while half >= 1:
            left = jnp.where((row_at // half) % 2 == 1, pltpu.roll(left, window - half, 2), left)
            half //= 2
        raws[me, h * per_half : (h + 1) * per_half] = jnp.sum(left, axis=1)[:, :taps]

    for r in peers:
        to_all(4, r).start()

    for r in peers:
        to_all(4, r).wait_recv()
    norms[line] = jnp.full(norms.shape[1:], jnp.sum(raws[...] * raws[...]), jnp.float32)
    for r in range(1, m):
        norm_copy(r).start()

    def products(returned, first, first_out, second, second_out):
        for d in range(n):
            cut = slice(d * cw, (d + 1) * cw)
            block = returned[d * pd : (d + 1) * pd].reshape(rows, cw)
            first_out[:, cut] = first[:, cut] * block
            second_out[:, cut] = second[:, cut] * block

    for r in peers:
        outward(2, r, conv_send, conv_ret).wait_recv()
    products(conv_ret, q_ref, go_ref, g_ref, gq_ref)
    for r in peers:
        outward(3, r, dmix_send, dmix_ret).wait_recv()
    products(dmix_ret, v_ref, gk_ref, k_ref, gv_ref)

    for r in range(1, m):
        norm_copy(r).wait_recv()
    squares = norms[0]
    for i in range(1, m):
        squares = squares + norms[i]
    factor = jnp.minimum(1.0, limit / jnp.sqrt(squares[0:1, :] + 1e-06))
    for d in range(n):
        fg_ref[d * groups : (d + 1) * groups, :] = raws[d] * factor[:, :taps]

    for kind, (source, target) in enumerate(
        ((mix_send, mix_recv), (gat_send, gat_recv), (conv_send, conv_ret), (dmix_send, dmix_ret))
    ):
        for r in peers:
            outward(kind, r, source, target).wait_send()
    for r in peers:
        to_all(4, r).wait_send()
    for r in range(1, m):
        norm_copy(r).wait_send()


def shards(n, m, query_rows, key_rows, value_rows, grad_rows, filters, span_order):
    rows, channels = query_rows.shape
    all_groups, taps = filters.shape
    group = channels // all_groups
    spans = span_order.shape[0]
    span_rows = rows * n // spans
    cw = channels // n
    lanes = min(128, cw)
    halves = cw // lanes
    groups = all_groups // n
    tokens = rows * n
    own = lax.dynamic_slice_in_dim(filters, lax.axis_index("seq") * groups, groups, 0)
    own = own.astype(jnp.float32)
    base = jnp.concatenate(
        [
            jnp.pad(own[:, ::-1], ((0, 0), (1, taps - 1))),
            jnp.pad(own, ((0, 0), (0, taps))),
        ],
        axis=0,
    )
    place = jnp.arange(spans, dtype=jnp.int32)
    held = span_order[None, :] == place[:, None]
    slots = jnp.sum(jnp.where(held, place[None, :], 0), axis=1, dtype=jnp.int32)
    block = pltpu.VMEM((spans, span_rows, cw), jnp.bfloat16)
    ordered = pltpu.VMEM((halves, tokens + taps, lanes), jnp.bfloat16)
    result = pltpu.VMEM((spans, halves, span_rows, lanes), jnp.bfloat16)
    vmem = pl.BlockSpec(memory_space=pltpu.VMEM)
    limit = math.sqrt(all_groups * m * taps)
    like = jax.ShapeDtypeStruct((rows, channels), jnp.bfloat16)
    return pl.pallas_call(
        functools.partial(kernel, n, m, taps, group, limit),
        out_shape=(like, like, like, like, jax.ShapeDtypeStruct((all_groups, taps), jnp.float32)),
        in_specs=[pl.BlockSpec(memory_space=pltpu.SMEM)] * 2 + [vmem] * 5,
        out_specs=(vmem,) * 5,
        scratch_shapes=[
            block, block, block, block, ordered, ordered, result, result,
            block, block, block, block,
            pltpu.VMEM((2 * groups, taps, 2 * taps), jnp.bfloat16),
            pltpu.VMEM((lanes // group, taps, 2 * taps), jnp.float32),
            pltpu.VMEM((n, groups, taps), jnp.float32),
            pltpu.VMEM((m, 8, 128), jnp.float32),
            pltpu.SemaphoreType.DMA((5, n)),
            pltpu.SemaphoreType.DMA((5, n)),
            pltpu.SemaphoreType.DMA((m,)),
            pltpu.SemaphoreType.DMA((m,)),
        ],
        compiler_params=pltpu.CompilerParams(
            collective_id=0, has_side_effects=True, vmem_limit_bytes=48 * 1024 * 1024
        ),
    )(span_order, slots, base, query_rows, key_rows, value_rows, grad_rows)


def solution(mesh):
    rows = P("seq", "chan")
    return jax.shard_map(
        functools.partial(shards, mesh.shape["seq"], mesh.shape["chan"]),
        mesh=mesh,
        in_specs=(rows, rows, rows, rows, P("chan", None), P()),
        out_specs=(rows, rows, rows, rows, P("chan", None)),
        check_vma=False,
    )
```

time: 485 us -> 46.3 us (0.10)
  blocking collectives: 163 us -> 0 us
  local copies, waits for them, and re-layouts: 166 us -> 8.69 us
  waiting for transfers between devices: 71.7 us -> 0 us
  Pallas kernels: 0 us -> 35.7 us
  matrix products: 27.3 us -> 0 us
  other arithmetic: 23 us -> 0.88 us
  starting transfers between devices: 16.8 us -> 0 us
  between operations: 15.1 us -> 0.66 us
    all_to_all x5 -> x0, blocking collectives: 151 us -> none  [the longest x1 31.6 us: shards(): lax.all_to_all(pack_rows(grad_rows, fill_slot, fill_valid, per_device), '...]
    gather x18 -> x0, local copies, waits for them, and re-layouts: 96.4 us -> none  [the longest x2 64 us: band_tables(): lookup = filters[:, offsets]]
    psum x1 -> x0, waiting for transfers between devices: 54.2 us -> none  [shards(): total_grad = lax.psum(partial_grad, 'seq')]
    pallas_call x0 -> x1, Pallas kernels: none -> 35.7 us  [shards(): pl.pallas_call(functools.partial(kernel, n, m, taps, group, limit), out_s...]
    reshape x2 -> x0, local copies, waits for them, and re-layouts: 35.3 us -> none  [the longest x1 17.8 us: filter_terms(): flattened = products.reshape(groups, 2 * taps * taps)]
    dot_general x5 -> x0, matrix products: 27.3 us -> none  [the longest x1 8.09 us: filter_terms(): jnp.einsum('tagc,tbgc->gab', grad_tiles, windows, preferred_element_type=...]
    all_to_all x3 -> x0, waiting for transfers between devices: 17.5 us -> none  [the longest x1 17.5 us: shards(): lax.all_to_all(pack_rows(value_rows, fill_slot, fill_valid, per_device),...]
    convert_element_type x9 -> x0, local copies, waits for them, and re-layouts: 14.9 us -> none  [the longest x2 7.37 us: times_rounded(): right.astype(jnp.float32)]
  transfers between devices with their start and end apart: 6 -> 0, of which waited for: 2 -> 0; matrix products, arithmetic and copies ran while one was open for 33% -> 0% of each run, Pallas kernels for 0% -> 0%
where the time goes in v1:
time: 46.3 us; the launch traced here: 45.9 us
  Pallas kernels  35.7 us (77%)
  local copies, waits for them, and re-layouts  8.69 us (19%)
  other arithmetic  0.88 us (2%)
  between operations  0.66 us (1%)
    pallas_call x1, Pallas kernels, shards(): pl.pallas_call(functools.partial(kernel, n, m, taps, group, limit), out_s...  35.7 us
    unnamed x15, local copies, waits for them, and re-layouts  8.62 us

profile of v1, /device:TPU:0, one launch (start us, length us, event | category | flops | bytes accessed | tf_op | source)
XLA Modules:
  0.0 45.9 jit_solution(12320014947549657902)
XLA Ops:
  0.6 0.0 copy-start.4
  0.6 0.6 %copy-done.4 = s32[16]{0:T(128)S(1)} copy-done((s32[16]{0:T(128)S(1)}, s32[16]{0:T(128)}, u32[]{:S(2)}) %copy-start.4) | copy-done | bytes 88
  1.3 0.1 select_reduce_fusion.slot_ref
  1.4 0.7 %dynamic-slice_convert_fusion = f32[16,128]{1,0:T(8,128)S(1)} fusion(bf16[128,128]{1,0:T(8,128)(2,1)} %param.10, s32[]{:T(128)S(6)} %select_n.8), kind=kLoop, calls=%fused_computation.5 | loop fusion | flops 2048 | bytes 12292 | tf_op jit(solution)/shard_map/convert_element_type | solution.py:269
  2.1 0.1 rev.3
  2.2 0.1 select_maximum_fusion.base_ref
  2.2 0.0 copy-start
  2.3 1.0 %copy-done = bf16[128,2048]{1,0:T(8,128)(2,1)S(1)} copy-done((bf16[128,2048]{1,0:T(8,128)(2,1)S(1)}, bf16[128,2048]{1,0:T(8,128)(2,1)}, u32[]{:S(2)}) %copy-start) | copy-done | bytes 524312
  3.3 0.0 copy-start.1
  3.3 1.0 %copy-done.1 = bf16[128,2048]{1,0:T(8,128)(2,1)S(1)} copy-done((bf16[128,2048]{1,0:T(8,128)(2,1)S(1)}, bf16[128,2048]{1,0:T(8,128)(2,1)}, u32[]{:S(2)}) %copy-start.1) | copy-done | bytes 524312
  4.3 0.0 copy-start.2
  4.3 1.0 %copy-done.2 = bf16[128,2048]{1,0:T(8,128)(2,1)S(1)} copy-done((bf16[128,2048]{1,0:T(8,128)(2,1)S(1)}, bf16[128,2048]{1,0:T(8,128)(2,1)}, u32[]{:S(2)}) %copy-start.2) | copy-done | bytes 524312
  5.4 0.0 copy-start.3
  5.4 1.0 %copy-done.3 = bf16[128,2048]{1,0:T(8,128)(2,1)S(1)} copy-done((bf16[128,2048]{1,0:T(8,128)(2,1)S(1)}, bf16[128,2048]{1,0:T(8,128)(2,1)}, u32[]{:S(2)}) %copy-start.3) | copy-done | bytes 524312
  6.4 35.7 %shard_map.101 = (bf16[128,2048]{1,0:T(8,128)(2,1)S(1)}, bf16[128,2048]{1,0:T(8,128)(2,1)S(1)}, bf16[128,2048]{1,0:T(8,128)(2,1)S(1)}, bf16[128,2048]{1,0:T(8,128)(2,1)S(1)}, f32[128,128]{1,0:T(8,128)S(1)}) custom-call(s32[16]{0:T(128)S(1)} %copy-done.4, s32[16]{0:T(128)S(1)} %select_reduce_fusion.slot_ref, f32[32,256]{1,0:T(8,128)S(1)} %select_maximum_fusion.base_ref, ...), custom_call_target="tpu_custom_call" | custom-call | tf_op jit(solution)/shard_map/pallas_call | solution.py:286
  42.1 0.8 %copy.16 = bf16[128,2048]{1,0:T(8,128)(2,1)} copy(bf16[128,2048]{1,0:T(8,128)(2,1)S(1)} %get-tuple-element.10) | data formatting | bytes 1048576
  42.9 0.8 %copy.17 = bf16[128,2048]{1,0:T(8,128)(2,1)} copy(bf16[128,2048]{1,0:T(8,128)(2,1)S(1)} %get-tuple-element.11) | data formatting | bytes 1048576
  43.7 0.8 %copy.18 = bf16[128,2048]{1,0:T(8,128)(2,1)} copy(bf16[128,2048]{1,0:T(8,128)(2,1)S(1)} %get-tuple-element.12) | data formatting | bytes 1048576
  44.5 0.8 %copy.19 = bf16[128,2048]{1,0:T(8,128)(2,1)} copy(bf16[128,2048]{1,0:T(8,128)(2,1)S(1)} %get-tuple-element.13) | data formatting | bytes 1048576
  45.3 0.6 %copy.20 = f32[128,128]{1,0:T(8,128)} copy(f32[128,128]{1,0:T(8,128)S(1)} %get-tuple-element.14) | data formatting | bytes 131072
Async XLA Ops:
  0.6 0.7 %copy-start.4 = (s32[16]{0:T(128)S(1)}, s32[16]{0:T(128)}, u32[]{:S(2)}) copy-start(s32[16]{0:T(128)} %order_ref.1) | copy-start | bytes 196
  2.2 1.0 %copy-start = (bf16[128,2048]{1,0:T(8,128)(2,1)S(1)}, bf16[128,2048]{1,0:T(8,128)(2,1)}, u32[]{:S(2)}) copy-start(bf16[128,2048]{1,0:T(8,128)(2,1)} %q_ref.1) | copy-start | bytes 1572868
  3.3 1.0 %copy-start.1 = (bf16[128,2048]{1,0:T(8,128)(2,1)S(1)}, bf16[128,2048]{1,0:T(8,128)(2,1)}, u32[]{:S(2)}) copy-start(bf16[128,2048]{1,0:T(8,128)(2,1)} %k_ref.1) | copy-start | bytes 1572868
  4.3 1.0 %copy-start.2 = (bf16[128,2048]{1,0:T(8,128)(2,1)S(1)}, bf16[128,2048]{1,0:T(8,128)(2,1)}, u32[]{:S(2)}) copy-start(bf16[128,2048]{1,0:T(8,128)(2,1)} %v_ref.1) | copy-start | bytes 1572868
  5.4 1.0 %copy-start.3 = (bf16[128,2048]{1,0:T(8,128)(2,1)S(1)}, bf16[128,2048]{1,0:T(8,128)(2,1)}, u32[]{:S(2)}) copy-start(bf16[128,2048]{1,0:T(8,128)(2,1)} %g_ref.1) | copy-start | bytes 1572868

commit v2 on v1

--- a/solution.py
+++ b/solution.py
@@ -23,11 +23,11 @@
 
 def kernel(
     n, m, taps, group, limit,
-    order_ref, slot_ref, base_ref, q_ref, k_ref, v_ref, g_ref,
+    order_ref, slot_ref, base_ref, q_in, k_in, v_in, g_in,
     go_ref, gq_ref, gk_ref, gv_ref, fg_ref,
     mix_send, gat_send, mix_recv, gat_recv, zseq, gseq, conv, dmix,
     conv_send, dmix_send, conv_ret, dmix_ret, bands, eacc, raws, norms,
-    send_sem, recv_sem, norm_send, norm_recv,
+    send_sem, recv_sem, norm_send, norm_recv, q_ref, k_ref, v_ref, g_ref, load_sem,
 ):
     me = lax.axis_index("seq")
     line = lax.axis_index("chan")
@@ -45,6 +45,14 @@
     per_tile = taps // span_rows
     peers = sorted(range(1, n), key=lambda r: (r & 1, -bin(r).count("1")))
 
+    loads = [
+        pltpu.make_async_copy(source, target, load_sem.at[i])
+        for i, (source, target) in enumerate(
+            ((k_in, k_ref), (v_in, v_ref), (g_in, g_ref), (q_in, q_ref))
+        )
+    ]
+    for load in loads:
+        load.start()
     barrier = pltpu.get_barrier_semaphore()
     for r in peers:
         pl.semaphore_signal(
@@ -89,10 +97,14 @@
             cut = slice(d * cw, (d + 1) * cw)
             out[d * pd : (d + 1) * pd] = (left[:, cut] * right[:, cut]).reshape(pd, span_rows, cw)
 
+    loads[0].wait()
+    loads[1].wait()
     blocks(k_ref, v_ref, mix_send)
     pl.semaphore_wait(barrier, n + m - 2)
     for r in peers:
         outward(0, r, mix_send, mix_recv).start()
+    loads[2].wait()
+    loads[3].wait()
     blocks(g_ref, q_ref, gat_send)
     for r in peers:
         outward(1, r, gat_send, gat_recv).start()
@@ -286,7 +298,9 @@
     return pl.pallas_call(
         functools.partial(kernel, n, m, taps, group, limit),
         out_shape=(like, like, like, like, jax.ShapeDtypeStruct((all_groups, taps), jnp.float32)),
-        in_specs=[pl.BlockSpec(memory_space=pltpu.SMEM)] * 2 + [vmem] * 5,
+        in_specs=[pl.BlockSpec(memory_space=pltpu.SMEM)] * 2
+        + [vmem]
+        + [pl.BlockSpec(memory_space=pl.ANY)] * 4,
         out_specs=(vmem,) * 5,
         scratch_shapes=[
             block, block, block, block, ordered, ordered, result, result,
@@ -299,6 +313,11 @@
             pltpu.SemaphoreType.DMA((5, n)),
             pltpu.SemaphoreType.DMA((m,)),
             pltpu.SemaphoreType.DMA((m,)),
+            pltpu.VMEM((rows, channels), jnp.bfloat16),
+            pltpu.VMEM((rows, channels), jnp.bfloat16),
+            pltpu.VMEM((rows, channels), jnp.bfloat16),
+            pltpu.VMEM((rows, channels), jnp.bfloat16),
+            pltpu.SemaphoreType.DMA((4,)),
         ],
         compiler_params=pltpu.CompilerParams(
             collective_id=0, has_side_effects=True, vmem_limit_bytes=48 * 1024 * 1024

time: 46.3 us -> 46.5 us (level)
  no operation moved by 1% of the time
where the time goes in v2:
time: 46.5 us; the launch traced here: 46.1 us
  Pallas kernels  35.9 us (77%)
  local copies, waits for them, and re-layouts  8.69 us (19%)
  other arithmetic  0.88 us (2%)
  between operations  0.66 us (1%)
    pallas_call x1, Pallas kernels, shards(): pl.pallas_call(functools.partial(kernel, n, m, taps, group, limit), out_s...  35.9 us
    unnamed x15, local copies, waits for them, and re-layouts  8.62 us

profile of v2, /device:TPU:0, one launch (start us, length us, event | category | flops | bytes accessed | tf_op | source)
XLA Modules:
  0.0 46.1 jit_solution(2800310301880707673)
XLA Ops:
  0.6 0.0 copy-start.4
  0.6 0.6 %copy-done.4 = s32[16]{0:T(128)S(1)} copy-done((s32[16]{0:T(128)S(1)}, s32[16]{0:T(128)}, u32[]{:S(2)}) %copy-start.4) | copy-done | bytes 88
  1.3 0.1 select_reduce_fusion.slot_ref
  1.4 0.7 %dynamic-slice_convert_fusion = f32[16,128]{1,0:T(8,128)S(1)} fusion(bf16[128,128]{1,0:T(8,128)(2,1)} %param.10, s32[]{:T(128)S(6)} %select_n.8), kind=kLoop, calls=%fused_computation.5 | loop fusion | flops 2048 | bytes 12292 | tf_op jit(solution)/shard_map/convert_element_type | solution.py:281
  2.1 0.1 rev.3
  2.2 0.1 select_maximum_fusion.base_ref
  2.2 0.0 copy-start
  2.3 1.0 %copy-done = bf16[128,2048]{1,0:T(8,128)(2,1)S(1)} copy-done((bf16[128,2048]{1,0:T(8,128)(2,1)S(1)}, bf16[128,2048]{1,0:T(8,128)(2,1)}, u32[]{:S(2)}) %copy-start) | copy-done | bytes 524312
  3.3 0.0 copy-start.1
  3.3 1.0 %copy-done.1 = bf16[128,2048]{1,0:T(8,128)(2,1)S(1)} copy-done((bf16[128,2048]{1,0:T(8,128)(2,1)S(1)}, bf16[128,2048]{1,0:T(8,128)(2,1)}, u32[]{:S(2)}) %copy-start.1) | copy-done | bytes 524312
  4.3 0.0 copy-start.2
  4.3 1.0 %copy-done.2 = bf16[128,2048]{1,0:T(8,128)(2,1)S(1)} copy-done((bf16[128,2048]{1,0:T(8,128)(2,1)S(1)}, bf16[128,2048]{1,0:T(8,128)(2,1)}, u32[]{:S(2)}) %copy-start.2) | copy-done | bytes 524312
  5.4 0.0 copy-start.3
  5.4 1.0 %copy-done.3 = bf16[128,2048]{1,0:T(8,128)(2,1)S(1)} copy-done((bf16[128,2048]{1,0:T(8,128)(2,1)S(1)}, bf16[128,2048]{1,0:T(8,128)(2,1)}, u32[]{:S(2)}) %copy-start.3) | copy-done | bytes 524312
  6.4 35.9 %shard_map.101 = (bf16[128,2048]{1,0:T(8,128)(2,1)S(1)}, bf16[128,2048]{1,0:T(8,128)(2,1)S(1)}, bf16[128,2048]{1,0:T(8,128)(2,1)S(1)}, bf16[128,2048]{1,0:T(8,128)(2,1)S(1)}, f32[128,128]{1,0:T(8,128)S(1)}) custom-call(s32[16]{0:T(128)S(1)} %copy-done.4, s32[16]{0:T(128)S(1)} %select_reduce_fusion.slot_ref, f32[32,256]{1,0:T(8,128)S(1)} %select_maximum_fusion.base_ref, ...), custom_call_target="tpu_custom_call" | custom-call | tf_op jit(solution)/shard_map/pallas_call | solution.py:298
  42.3 0.8 %copy.16 = bf16[128,2048]{1,0:T(8,128)(2,1)} copy(bf16[128,2048]{1,0:T(8,128)(2,1)S(1)} %get-tuple-element.10) | data formatting | bytes 1048576
  43.1 0.8 %copy.17 = bf16[128,2048]{1,0:T(8,128)(2,1)} copy(bf16[128,2048]{1,0:T(8,128)(2,1)S(1)} %get-tuple-element.11) | data formatting | bytes 1048576
  43.9 0.8 %copy.18 = bf16[128,2048]{1,0:T(8,128)(2,1)} copy(bf16[128,2048]{1,0:T(8,128)(2,1)S(1)} %get-tuple-element.12) | data formatting | bytes 1048576
  44.7 0.8 %copy.19 = bf16[128,2048]{1,0:T(8,128)(2,1)} copy(bf16[128,2048]{1,0:T(8,128)(2,1)S(1)} %get-tuple-element.13) | data formatting | bytes 1048576
  45.5 0.6 %copy.20 = f32[128,128]{1,0:T(8,128)} copy(f32[128,128]{1,0:T(8,128)S(1)} %get-tuple-element.14) | data formatting | bytes 131072
Async XLA Ops:
  0.6 0.7 %copy-start.4 = (s32[16]{0:T(128)S(1)}, s32[16]{0:T(128)}, u32[]{:S(2)}) copy-start(s32[16]{0:T(128)} %order_ref.1) | copy-start | bytes 196
  2.2 1.0 %copy-start = (bf16[128,2048]{1,0:T(8,128)(2,1)S(1)}, bf16[128,2048]{1,0:T(8,128)(2,1)}, u32[]{:S(2)}) copy-start(bf16[128,2048]{1,0:T(8,128)(2,1)} %q_in.1) | copy-start | bytes 1572868
  3.3 1.0 %copy-start.1 = (bf16[128,2048]{1,0:T(8,128)(2,1)S(1)}, bf16[128,2048]{1,0:T(8,128)(2,1)}, u32[]{:S(2)}) copy-start(bf16[128,2048]{1,0:T(8,128)(2,1)} %k_in.1) | copy-start | bytes 1572868
  4.3 1.0 %copy-start.2 = (bf16[128,2048]{1,0:T(8,128)(2,1)S(1)}, bf16[128,2048]{1,0:T(8,128)(2,1)}, u32[]{:S(2)}) copy-start(bf16[128,2048]{1,0:T(8,128)(2,1)} %v_in.1) | copy-start | bytes 1572868
  5.4 1.0 %copy-start.3 = (bf16[128,2048]{1,0:T(8,128)(2,1)S(1)}, bf16[128,2048]{1,0:T(8,128)(2,1)}, u32[]{:S(2)}) copy-start(bf16[128,2048]{1,0:T(8,128)(2,1)} %g_in.1) | copy-start | bytes 1572868
